TPU v7x, 512 devices: a whole 4x8x8 slice. The times are simulated.
512 devices in a mesh: walker: 128 (over z, y, core), space: 4 (over x).
Axes of the slice: x: 4, y: 8, z: 8, core: 2. Of those that a mesh axis runs over, the one named last changes fastest.
Arguments:
- positions: float32 [128, 3, 12288], P('walker', None, 'space'), may hold values from -6 to 6
- velocities: float32 [128, 3, 12288], P('walker', None, 'space'), may hold values from -6 to 6
- weights: float32 [128], P('walker'), may hold values from 0.2 to 2
- strength: float32 [12288], P('space'), may hold values from 0.3 to 3
- tiles: int32 [96, 27], P('space'), may hold values from 0 to 27, as said below
- plan: int32 [128], replicated, may hold values from 0 to 127
- home: int32 [128], replicated, may hold values from 0 to 127, as said below
Outputs:
- distances: float32 [128, 128], P('walker', 'space')
- new_positions: float32 [128, 3, 12288], P('walker', None, 'space')
- new_velocities: float32 [128, 3, 12288], P('walker', None, 'space')
- new_weights: float32 [128], P('walker')
Inputs may be any that keep to these rules, and one draw needn't show every extreme that they name: tiles[g, k] - 2 + (g // 24) * 24 is a cell inside the walker's grid at most 2 cells from g; entries 1 and 2 of each list are the cells 2 before and 2 after g, or the nearest end cell where those do not exist; entries may repeat. home is a permutation.
All inputs are finite; a program needn't handle non-finite values.
Results may differ from a plain program's by a relative error of at most 0.0003.
Values may be sent and summed in bfloat16 or wider, within the bound.
A program may use at most 64 MiB of HBM per device.

v0:
```python
import jax
import jax.numpy as jnp
from jax import lax
from jax.sharding import PartitionSpec as P

NBR = 27
HALO = 2
SITES = 8192


STEP = 0.1


def with_halo(block, sides, width):
    for axis, dim in sides:
        count = lax.axis_size(axis)
        forward = [(i, i + 1) for i in range(count - 1)]
        backward = [(target, source) for source, target in forward]
        low = lax.ppermute(
            lax.slice_in_dim(block, block.shape[dim] - width, None, axis=dim), axis, forward
        )
        high = lax.ppermute(lax.slice_in_dim(block, 0, width, axis=dim), axis, backward)
        block = jnp.concatenate([low, block, high], axis=dim)
    return block


def tile_force(pos, near, near_str):
    delta = pos[..., :, None] - near[..., None, :]
    radius = jnp.sum(delta * delta, axis=1)
    factor = near_str[:, None, :] / jnp.square(1.0 + radius)
    return jnp.sum(factor[:, None] * delta, axis=-1)


def forces(pos, ext_pos, ext_str, str_loc, table):

    def turn(k, total):
        column = lax.dynamic_index_in_dim(table, k, 1, keepdims=False)
        near = jnp.take(ext_pos, column, axis=2)
        near_str = jnp.take(ext_str, column, axis=0)
        return total + tile_force(pos, near, near_str)

    total = lax.fori_loop(0, NBR, turn, jnp.zeros(pos.shape, jnp.float32))
    return str_loc * total


def extend(field):
    return with_halo(field, (("space", 1),), HALO)


def advance(pos, vel, str_cells, tiles):
    count, cells, per_tile = (pos.shape[0], str_cells.shape[0], str_cells.shape[1])
    rows = jnp.concatenate([pos.reshape(count * 3, cells, per_tile), str_cells[None]], axis=0)
    widened = extend(rows)
    ext_str = widened[count * 3]
    ext_pos = widened[: count * 3].reshape(count, 3, -1, per_tile)
    force = forces(pos, ext_pos, ext_str, str_cells, tiles)
    vel = vel + STEP * force
    pos = pos + STEP * vel
    ext_pos = extend(pos.reshape(count * 3, cells, per_tile)).reshape(count, 3, -1, per_tile)
    force = forces(pos, ext_pos, ext_str, str_cells, tiles)
    vel = vel + STEP * force
    pos = pos + STEP * vel
    return (pos, vel)


def site_features(pos_flat, site_dev):
    return pos_flat[..., :site_dev].astype(jnp.bfloat16)


def shards(positions, velocities, weights, strength, tiles, plan, home):
    cells = tiles.shape[0]
    atoms = strength.shape[0]
    per_tile = atoms // cells
    walkers = plan.shape[0]
    site_dev = SITES // lax.axis_size("space")
    slot = lax.axis_index("walker")
    labels = jnp.arange(walkers, dtype=jnp.int32)
    chosen = plan[:, None] == labels[None, :]
    source_rows = jnp.sum(jnp.where(chosen, home[None, :], 0), axis=1)
    counts = jnp.sum((plan[:, None] == plan[None, :]).astype(jnp.int32), axis=1)
    mine = labels == slot
    my_source = jnp.sum(jnp.where(mine, source_rows, 0))
    my_count = jnp.sum(jnp.where(mine, counts, 0)).astype(jnp.float32)
    str_cells = strength.reshape(cells, per_tile)
    start_pos, start_vel = (positions, velocities)
    count = start_pos.shape[0]
    moved_pos, moved_vel = advance(
        start_pos.reshape(count, 3, cells, per_tile),
        start_vel.reshape(count, 3, cells, per_tile),
        str_cells,
        tiles,
    )
    moved_pos = moved_pos.reshape(count, 3, atoms)
    moved_vel = moved_vel.reshape(count, 3, atoms)
    own_features = site_features(moved_pos[0], site_dev).reshape(-1)
    own_values = own_features.astype(jnp.float32)
    diff = own_values[None, :] - lax.all_gather(
        own_features[None], "walker", axis=0, tiled=True
    ).astype(jnp.float32)
    row = jnp.sum(diff * diff, axis=1)
    piece = (
        lax.all_gather(moved_pos, "walker", axis=0, tiled=True),
        lax.all_gather(moved_vel, "walker", axis=0, tiled=True),
        lax.all_gather(weights, "walker", axis=0, tiled=True),
    )
    size = piece[0].shape[0]
    hit = (jnp.arange(size, dtype=jnp.int32) == my_source).astype(jnp.float32)
    picked_pos = jnp.sum(hit[:, None, None] * piece[0], axis=0)
    picked_vel = jnp.sum(hit[:, None, None] * piece[1], axis=0)
    picked_weight = jnp.sum(hit * piece[2])
    partial_value = lax.psum_scatter(row[None], "space", scatter_dimension=1, tiled=True)
    distances = partial_value / (3.0 * SITES)
    new_weights = (picked_weight / my_count)[None]
    return (distances, picked_pos[None], picked_vel[None], new_weights)


def solution(mesh):
    return jax.shard_map(
        shards,
        mesh=mesh,
        in_specs=(
            P("walker", None, "space"),
            P("walker", None, "space"),
            P("walker"),
            P("space"),
            P("space", None),
            P(),
            P(),
        ),
        out_specs=(
            P("walker", "space"),
            P("walker", None, "space"),
            P("walker", None, "space"),
            P("walker"),
        ),
        check_vma=False,
    )
```

profile of v0, /device:TPU:1, one launch (start us, length us, event | category | flops | bytes accessed | tf_op | source)
XLA Modules:
  0.0 727.6 jit_solution(16970784414580283710)
XLA Ops:
  8.0 3.9 collective-permute-start
  17.8 164.5 %while.28 = (s32[]{:T(128)}, f32[1,3,24,128]{3,2,1,0:T(8,128)S(1)}, s32[24,27]{0,1:T(8,128)S(1)}, f32[28,128]{1,0:T(8,128)S(1)}, f32[1,3,3072]{2,1,0:T(4,128)S(1...) while((s32[]{:T(128)}, f32[1,3,24,128]{3,2,1,0:T(8,128)S(1)}, ...), condition=%wide.region_3.0_spmd.clone, body=%wide.region_0.5_spmd.clone.sunk | while | flops 7886995 | bytes 6947475 | solution.py:42
  19.2 1.6 fusion.20
  21.0 2.9 fusion.21
  27.1 2.9 fusion.21
  33.2 2.9 fusion.21
  39.3 2.9 fusion.21
  45.4 2.9 fusion.21
  51.5 2.9 fusion.21
  57.6 2.9 fusion.21
  63.7 2.9 fusion.21
  69.8 2.9 fusion.21
  75.9 2.9 fusion.21
  82.0 2.9 fusion.21
  88.1 2.9 fusion.21
  94.2 2.9 fusion.21
  100.3 2.9 fusion.21
  106.3 2.9 fusion.21
  112.4 2.9 fusion.21
  118.5 2.9 fusion.21
  124.6 2.9 fusion.21
  130.7 2.9 fusion.21
  136.8 2.9 fusion.21
  142.9 2.9 fusion.21
  149.0 2.9 fusion.21
  155.1 2.9 fusion.21
  161.2 2.9 fusion.21
  167.3 2.9 fusion.21
  173.4 2.9 fusion.21
  179.5 2.9 fusion.21
  182.4 3.1 collective-permute-start.2
  186.9 3.0 collective-permute-done.3
  190.0 164.9 %while.29 = (s32[]{:T(128)}, f32[1,3,24,128]{3,2,1,0:T(8,128)S(1)}, s32[24,27]{0,1:T(8,128)S(1)}, f32[28,128]{1,0:T(8,128)S(1)}, f32[1,3,24,128]{3,2,1,0:T(8,128...) while((s32[]{:T(128)}, f32[1,3,24,128]{3,2,1,0:T(8,128)S(1)}, ...), condition=%wide.region_7.10_spmd.clone, body=%wide.region_4.9_spmd.clone.sunk | while | flops 7886995 | bytes 6873747 | solution.py:42
  193.2 2.9 fusion.24
  199.3 2.9 fusion.24
  205.4 2.9 fusion.24
  211.5 2.9 fusion.24
  217.6 2.9 fusion.24
  223.7 2.9 fusion.24
  229.8 2.9 fusion.24
  235.9 2.9 fusion.24
  242.0 2.9 fusion.24
  248.1 2.9 fusion.24
  254.2 2.9 fusion.24
  260.3 2.9 fusion.24
  266.5 2.9 fusion.24
  272.6 2.9 fusion.24
  278.7 2.9 fusion.24
  284.8 2.9 fusion.24
  290.9 2.9 fusion.24
  297.0 2.9 fusion.24
  303.1 2.9 fusion.24
  309.2 2.9 fusion.24
  315.3 2.9 fusion.24
  321.4 2.9 fusion.24
  327.5 2.9 fusion.24
  333.6 2.9 fusion.24
  339.7 2.9 fusion.24
  345.9 2.9 fusion.24
  352.0 2.9 fusion.24
  355.7 90.0 %all-gather.9.cloned.1.call-done = bf16[128,1,6144]{2,1,0:T(2,128)(2,1)} async-done(((bf16[1,1,6144]{2,1,0:T(2,128)(2,1)}), bf16[128,1,6144]{2,1,0:T(2,128)(2,1)}) %all-gather.9.cloned.1.call-update) | async-done | bytes 1572880 | tf_op jit(solution)/shard_map/all_gather | solution.py:97
  445.7 5.1 convert_element_type.34
  458.4 247.5 %all-reduce = f32[128]{0:T(128)S(1)} all-reduce(f32[128]{0:T(128)S(1)} %dynamic-update-slice), channel_id=1, replica_groups=mesh['walker'=128,'space'=4] {'walker'}, use_global_device_ids=true, to_apply=%add | all-reduce | flops 128 | bytes 1024
  710.4 8.2 %multiply_reduce_fusion = (f32[3,3072]{1,0:T(4,128)S(1)}, f32[3,3072]{1,0:T(4,128)S(1)}) fusion(f32[128,3,3072]{2,1,0:T(4,128)} %all-gather.7.cloned.1.call-done, f32[128]{0:T(128)S(1)} %compare_convert_fusion, f32[128,3,3072]{2,1,0:T(4,128)} %all-gather.5.cloned.1.call-done), kind=kLoop, calls=%fused_computation.29 | loop fusion | flops 4700160 | bytes 9511424 | tf_op jit(solution)/shard_map/reduce_sum | solution.py:109
  (625 shorter events, 189.1 us)
Async XLA Ops:
  7.2 438.5 %all-gather.9.cloned.1.call-start = ((), (), s32[]{:S(2)}) async-start(), calls=%async_computation.3 | async-start | bytes 3170304 | tf_op jit(solution)/shard_map/all_gather | solution.py:97
  8.0 6.8 collective-permute-start
  11.9 4.4 collective-permute-start.1
  17.8 164.6 %copy-start = (f32[1,3,3072]{2,0,1:T(1,128)S(1)}, f32[1,3,3072]{2,0,1:T(1,128)}, u32[]{:S(2)}) copy-start(f32[1,3,3072]{2,0,1:T(1,128)} %param.15) | copy-start | bytes 110596
  17.8 164.6 %copy-start.1 = (f32[3072]{0:T(1024)S(1)}, f32[3072]{0:T(1024)}, u32[]{:S(2)}) copy-start(f32[3072]{0:T(1024)} %param.18) | copy-start | bytes 36868
  17.8 164.6 %copy-start.2 = (f32[1,3,3072]{2,0,1:T(1,128)S(1)}, f32[1,3,3072]{2,0,1:T(1,128)}, u32[]{:S(2)}) copy-start(f32[1,3,3072]{2,0,1:T(1,128)} %param.16) | copy-start | bytes 110596
  182.4 4.4 collective-permute-start.2
  185.6 4.3 collective-permute-start.3
  355.6 353.5 %reduce-scatter.4.cloned.1.call-start = ((), (), s32[]{:S(2)}) async-start(), calls=%async_computation.4 | async-start | bytes 81920
  450.8 4.1 copy-start.3
  450.8 4.1 copy-start.4
  452.8 257.6 %all-gather.5.cloned.1.call-start = ((), (), s32[]{:S(2)}) async-start(), calls=%async_computation.1 | async-start | bytes 6340608 | tf_op jit(solution)/shard_map/all_gather | solution.py:102
  453.6 256.9 %all-gather.7.cloned.1.call-start = ((), (), s32[]{:S(2)}) async-start(), calls=%async_computation.2 | async-start | bytes 6340608 | tf_op jit(solution)/shard_map/all_gather | solution.py:103
Sparse Core Ops, SparseCore 0:
  355.7 89.9 all-gather.8
  453.0 19.9 reduce-scatter.3
  476.6 88.9 all-gather.4
  569.0 83.4 all-gather.6
where the time goes:
time: 730 us; the launch traced here: 728 us
  other arithmetic  283 us (39%)
  blocking collectives  247 us (34%)
  waiting for transfers between devices  94.6 us (13%)
  local copies, waits for them, and re-layouts  71.6 us (10%)
  between operations  17.1 us (2%)
  starting transfers between devices  9.8 us (1%)
    unnamed x1, blocking collectives  247 us
    reduce_sum x54, other arithmetic, tile_force(): return jnp.sum(factor[:, None] * delta, axis=-1)  155 us
    all_gather x1, waiting for transfers between devices, shards(): lax.all_gather(own_features[None], 'walker', axis=0, tiled=True)  90 us
    reduce_sum x54, other arithmetic, tile_force(): radius = jnp.sum(delta * delta, axis=1)  84 us
    gather x54, local copies, waits for them, and re-layouts, turn(): near = jnp.take(ext_pos, column, axis=2)  32.2 us
    gather x54, local copies, waits for them, and re-layouts, turn(): near_str = jnp.take(ext_str, column, axis=0)  30.7 us
  transfers between devices with their start and end apart: 8, of which 3 were waited for; matrix products, arithmetic and copies ran while one was open for 1% of the time, Pallas kernels for 0%

commit v1 on v0

v1 whole, which is shorter than its diff:
```python
import functools

import jax
import jax.numpy as jnp
from jax import lax
from jax.experimental import pallas as pl
from jax.experimental.pallas import tpu as pltpu
from jax.sharding import PartitionSpec as P

HALO = 2
REACH = 2 * HALO + 1
SITES = 8192
STEP = 0.1
TILE = 128
ROWS = 40
MESH = pl.DeviceIdType.MESH


def kernel(
    n,
    nx,
    sites,
    pos,
    vel,
    stg,
    til,
    planv,
    wgt,
    plan,
    home,
    dist,
    npos,
    nvel,
    nwt,
    cast_a,
    cast_b,
    cast_s,
    mult,
    x1,
    v1,
    low_p,
    high_p,
    low_s,
    high_s,
    low_n,
    high_n,
    stage_x,
    stage_v,
    feat,
    feat_in,
    group,
    wide,
    own_rows,
    part,
    part_in,
    line,
    held_x,
    held_v,
    pick_x,
    pick_v,
    take_x,
    take_v,
    give_x,
    give_v,
    got_x,
    got_v,
    halo_send,
    halo_recv,
    f1_send,
    f1_recv,
    f2_send,
    f2_recv,
    f4_send,
    f4_recv,
    f5_send,
    f5_recv,
    s0_send,
    s0_recv,
    s1_send,
    s1_recv,
    s2_send,
    s2_recv,
    s3_send,
    s3_recv,
):
    cells = pos.shape[1]
    half = cells // 2
    members = 2 * n
    me = lax.axis_index("walker")
    here = lax.axis_index("space")
    core = me % 2
    yy = (me // 2) % n
    zz = me // members
    mine = me % members

    first = zz + core * (yy - zz)
    second = yy + core * (zz - yy)
    first_stride = 2 * (n - (n - 1) * core)
    second_stride = 2 * (1 + (n - 1) * core)
    pair = 1 - core
    twin = me + pair - core

    def member(m):
        return (zz * members + m, here)

    def level(z):
        return (z * members + mine, here)

    def along_first(p):
        return (p * first_stride + second * second_stride + core, here)

    def along_second(q):
        return (first * first_stride + q * second_stride + core, here)

    right = (me, (here + 1) % nx)
    left = (me, (here + nx - 1) % nx)

    barrier = pltpu.get_barrier_semaphore()

    def hello_member(k, _):
        pl.semaphore_signal(
            barrier, inc=1, device_id=member((mine + k) % members), device_id_type=MESH
        )
        return 0

    def hello_level(k, _):
        pl.semaphore_signal(
            barrier, inc=1, device_id=level((zz + k) % n), device_id_type=MESH
        )
        return 0

    def hello_space(k, _):
        pl.semaphore_signal(
            barrier, inc=1, device_id=(me, (here + k) % nx), device_id_type=MESH
        )
        return 0

    lax.fori_loop(1, nx, hello_space, 0)
    lax.fori_loop(1, members, hello_member, 0)
    lax.fori_loop(1, n, hello_level, 0)

    def remote(src, dst, send, recv, where):
        return pltpu.make_async_remote_copy(
            src_ref=src,
            dst_ref=dst,
            send_sem=send,
            recv_sem=recv,
            device_id=where,
            device_id_type=MESH,
        )

    rows = lax.broadcasted_iota(jnp.int32, til.shape, 0)
    shift = til[...] - rows
    for o in range(REACH):
        hits = jnp.sum((shift == o).astype(jnp.float32), axis=1, keepdims=True)
        mult[o] = jnp.broadcast_to(hits, (cells, TILE))

    def spread(dst, block, d, start):
        turned = block.T
        for g in range(block.shape[0]):
            value = jnp.broadcast_to(turned[:, g : g + 1], (TILE, TILE))
            if d is None:
                dst[start + g] = value
            else:
                dst[d, start + g] = value

    for d in range(3):
        spread(cast_a, pos[d], d, HALO)
    spread(cast_s, stg[...], None, HALO)

    def force(cast, source, g):
        at = [source[d, pl.ds(g, 1), :] for d in range(3)]
        total = [jnp.zeros((8, TILE), jnp.float32) for _ in range(3)]
        for o in range(REACH):
            acc = None
            for b in range(TILE // 32):
                piece = pl.ds(32 * b, 32)
                delta = [at[d] - cast[d, g + o, piece, :] for d in range(3)]
                q = delta[0] * delta[0] + 1.0
                q = q + delta[1] * delta[1]
                q = q + delta[2] * delta[2]
                w = pltpu.reciprocal(q * q, approx=True) * cast_s[g + o, piece, :]
                terms = [w * delta[d] for d in range(3)]
                if acc is None:
                    acc = terms
                else:
                    acc = [acc[d] + terms[d] for d in range(3)]
            count = mult[o, pl.ds(g, 1), :]
            for d in range(3):
                folded = acc[d][0:8] + acc[d][8:16] + (acc[d][16:24] + acc[d][24:32])
                total[d] = total[d] + count * folded
        weight = stg[pl.ds(g, 1), :]
        return [
            weight * jnp.sum(total[d], axis=0, keepdims=True) for d in range(3)
        ]

    def first_step(g):
        f = force(cast_a, pos, g)
        h = g // half
        for d in range(3):
            v = vel[d, pl.ds(g, 1), :] + STEP * f[d]
            x = pos[d, pl.ds(g, 1), :] + STEP * v
            v1[d, pl.ds(g, 1), :] = v
            x1[d, pl.ds(g, 1), :] = x
            stage_x[h, pl.ds(d * half + g - h * half, 1), :] = x

    def second_step(g, site):
        f = force(cast_b, x1, g)
        h = g // half
        for d in range(3):
            v = v1[d, pl.ds(g, 1), :] + STEP * f[d]
            x = x1[d, pl.ds(g, 1), :] + STEP * v
            stage_v[h, pl.ds(d * half + g - h * half, 1), :] = v
            if site:
                feat[g, pl.ds(d, 1), :] = x
        if site:

            @pl.when(g != mine)
            def _():
                remote(
                    feat.at[g],
                    feat_in.at[mine],
                    f1_send.at[g],
                    f1_recv.at[mine],
                    member(g),
                ).start()

    def run(step, low, high, turn=lambda k: k):
        def body(k, _):
            step(turn(k))
            return 0

        lax.fori_loop(low, high, body, 0)

    for h in range(2):
        stage_x[h, pl.ds(3 * half, ROWS - 3 * half), :] = jnp.broadcast_to(
            wgt[0], (ROWS - 3 * half, TILE)
        )
        stage_v[h, pl.ds(3 * half, ROWS - 3 * half), :] = jnp.zeros(
            (ROWS - 3 * half, TILE), jnp.float32
        )
    feat[...] = jnp.zeros(feat.shape, jnp.float32)

    run(first_step, HALO, 6)

    pl.semaphore_wait(barrier, (nx - 1) + (members - 1) + (n - 1))

    top = cells - 8
    halos = [
        remote(pos.at[:, pl.ds(top, 8), :], low_p, halo_send.at[0], halo_recv.at[0], right),
        remote(pos.at[:, pl.ds(0, 8), :], high_p, halo_send.at[1], halo_recv.at[1], left),
        remote(stg.at[pl.ds(top, 8), :], low_s, halo_send.at[2], halo_recv.at[2], right),
        remote(stg.at[pl.ds(0, 8), :], high_s, halo_send.at[3], halo_recv.at[3], left),
    ]
    for copy in halos:
        copy.start()

    run(first_step, 6, cells - HALO)

    for copy in halos:
        copy.wait()
    for d in range(3):
        spread(cast_a, low_p[d, 8 - HALO : 8, :], d, 0)
        spread(cast_a, high_p[d, 0:HALO, :], d, HALO + cells)
    spread(cast_s, low_s[8 - HALO : 8, :], None, 0)
    spread(cast_s, high_s[0:HALO, :], None, HALO + cells)

    run(first_step, 0, 2 * HALO, lambda k: k + (k // HALO) * (cells - 2 * HALO))

    nexts = [
        remote(x1.at[:, pl.ds(top, 8), :], low_n, halo_send.at[4], halo_recv.at[4], right),
        remote(x1.at[:, pl.ds(0, 8), :], high_n, halo_send.at[5], halo_recv.at[5], left),
    ]
    for copy in nexts:
        copy.start()

    slot_of_twin = 2 * second + core
    slot_of_pair = 2 * first + pair

    def to_twin(a, stage, held):
        return remote(
            stage.at[pair],
            held.at[slot_of_twin],
            s0_send.at[a],
            s0_recv.at[a],
            (twin, here),
        )

    def from_twin(a, stage, held):
        return remote(
            stage.at[pair],
            held.at[slot_of_pair],
            s0_send.at[a],
            s0_recv.at[a],
            (twin, here),
        )

    def out_first(a, held, p):
        return remote(
            held.at[pl.ds(2 * first, 2)],
            held.at[pl.ds(2 * first, 2)],
            s1_send.at[a * n + p],
            s1_recv.at[a * n + first],
            along_first(p),
        )

    def in_first(a, held, p):
        return remote(
            held.at[pl.ds(2 * p, 2)],
            held.at[pl.ds(2 * p, 2)],
            s1_send.at[a * n + p],
            s1_recv.at[a * n + p],
            along_first(p),
        )

    def out_second(a, pick, take, q):
        return remote(
            pick.at[q],
            take.at[second],
            s2_send.at[a * n + q],
            s2_recv.at[a * n + second],
            along_second(q),
        )

    def in_second(a, pick, take, q):
        return remote(
            pick.at[q],
            take.at[q],
            s2_send.at[a * n + q],
            s2_recv.at[a * n + q],
            along_second(q),
        )

    def others(count, own, act):
        def body(k, _):
            act((own + k) % count)
            return 0

        lax.fori_loop(1, count, body, 0)

    def source_parts(slot):
        row = home[plan[slot]]
        z = row // members
        y = (row // 2) % n
        c = row % 2
        return z + core * (y - z), y + core * (z - y), c

    def begin(a, stage, held):
        to_twin(a, stage, held).start()
        held[2 * first + core] = stage[core]

    def gather(a, stage, held):
        from_twin(a, stage, held).wait_recv()
        others(n, first, lambda p: out_first(a, held, p).start())

    def scatter(a, held, pick, take):
        others(n, first, lambda p: in_first(a, held, p).wait_recv())

        def choose(q, _):
            for c in range(2):
                slot = first * first_stride + q * second_stride + c
                p_src, _, c_src = source_parts(slot)
                pick[q, c] = held[2 * p_src + c_src]
            return 0

        lax.fori_loop(0, n, choose, 0)
        others(n, second, lambda q: out_second(a, pick, take, q).start())
        take[second] = pick[second]

    def finish(a, pick, take, give, got):
        others(n, second, lambda q: in_second(a, pick, take, q).wait_recv())
        _, q_twin, _ = source_parts(twin)
        give[...] = take[q_twin, pair]
        copy = remote(give, got, s3_send.at[a], s3_recv.at[a], (twin, here))
        copy.start()

    for d in range(3):
        spread(cast_b, x1[d], d, HALO)
    begin(0, stage_x, held_x)

    early = members - 2 * HALO
    run(lambda g: second_step(g, True), HALO, early)
    gather(0, stage_x, held_x)
    run(lambda g: second_step(g, True), early, members)

    for copy in nexts:
        copy.wait()
    for d in range(3):
        spread(cast_b, low_n[d, 8 - HALO : 8, :], d, 0)
        spread(cast_b, high_n[d, 0:HALO, :], d, HALO + cells)
    run(lambda g: second_step(g, True), 0, HALO)
    run(lambda g: second_step(g, False), members, cells - 2 * HALO)

    def f1(m):
        return remote(
            feat.at[m], feat_in.at[m], f1_send.at[m], f1_recv.at[m], member(m)
        )

    def f2(z):
        return remote(group.at[zz], group.at[zz], f2_send.at[z], f2_recv.at[zz], level(z))

    def f2_in(z):
        return remote(group.at[z], group.at[z], f2_send.at[z], f2_recv.at[z], level(z))

    feat_in[mine] = feat[mine]
    others(members, mine, lambda m: f1(m).wait_recv())
    for d in range(3):
        group[zz, :, TILE * d : TILE * (d + 1)] = feat_in[:, d, :].astype(jnp.bfloat16)
    others(n, zz, lambda z: f2(z).start())

    scatter(0, held_x, pick_x, take_x)
    run(lambda g: second_step(g, False), cells - 2 * HALO, cells)
    begin(1, stage_v, held_v)
    gather(1, stage_v, held_v)

    others(n, zz, lambda z: f2_in(z).wait_recv())
    walkers = n * members
    wide[...] = group[...].astype(jnp.float32).reshape(walkers, 3 * TILE)
    for d in range(3):
        own_rows[d] = group[zz, :, TILE * d : TILE * (d + 1)].astype(jnp.float32)
    lanes = lax.broadcasted_iota(jnp.int32, (walkers, TILE), 1)

    def row_of(r, acc):
        total = None
        for d in range(3):
            part_of = pl.ds(TILE * d, TILE)
            diff = wide[:, part_of] - own_rows[d, pl.ds(r, 1), :]
            square = diff * diff
            total = square if total is None else total + square
        return jnp.where(lanes == r, jnp.sum(total, axis=1, keepdims=True), acc)

    sums = lax.fori_loop(0, members, row_of, jnp.zeros((walkers, TILE), jnp.float32)).T
    for r in range(members):
        part[r, :, 0:walkers] = jnp.broadcast_to(sums[r : r + 1], (8, walkers))

    def f4(m):
        return remote(
            part.at[m], part_in.at[mine], f4_send.at[m], f4_recv.at[mine], member(m)
        )

    def f4_in(m):
        return remote(part.at[m], part_in.at[m], f4_send.at[m], f4_recv.at[m], member(m))

    others(members, mine, lambda m: f4(m).start())
    part_in[mine] = part[mine]

    finish(0, pick_x, take_x, give_x, got_x)
    others(members, mine, lambda m: f4_in(m).wait_recv())
    row = part_in[0]
    for m in range(1, members):
        row = row + part_in[m]
    line[here] = row

    def f5(s):
        return remote(
            line.at[here], line.at[here], f5_send.at[s], f5_recv.at[here], (me, s)
        )

    def f5_in(s):
        return remote(line.at[s], line.at[s], f5_send.at[s], f5_recv.at[s], (me, s))

    others(nx, here, lambda s: f5(s).start())

    scatter(1, held_v, pick_v, take_v)

    others(nx, here, lambda s: f5_in(s).wait_recv())
    row = line[0, 0:1, 0:walkers]
    for s in range(1, nx):
        row = row + line[s, 0:1, 0:walkers]
    row = row / (3.0 * sites)
    share = walkers // nx
    mine_of = row[:, 0:share]
    for s in range(1, nx):
        mine_of = jnp.where(here == s, row[:, share * s : share * (s + 1)], mine_of)
    dist[...] = mine_of

    finish(1, pick_v, take_v, give_v, got_v)

    _, q_own, _ = source_parts(me)
    own_x = take_x[q_own, core]
    own_v = take_v[q_own, core]
    same = (planv[...] == plan[me]).astype(jnp.float32)
    nwt[...] = own_x[3 * half : 3 * half + 1, 0:1] / jnp.sum(same, axis=1, keepdims=True)

    def other_half(a, give, got):
        return remote(give, got, s3_send.at[a], s3_recv.at[a], (twin, here))

    other_half(0, give_x, got_x).wait_recv()
    other_half(1, give_v, got_v).wait_recv()
    far_x = got_x[...]
    far_v = got_v[...]
    for h in range(2):
        v = jnp.where(core == h, own_v, far_v)
        x = jnp.where(core == h, own_x, far_x) + STEP * v
        for d in range(3):
            nvel[d, half * h : half * (h + 1), :] = v[half * d : half * (d + 1)]
            npos[d, half * h : half * (h + 1), :] = x[half * d : half * (d + 1)]

    for a, stage, held, pick, take, give, got in (
        (0, stage_x, held_x, pick_x, take_x, give_x, got_x),
        (1, stage_v, held_v, pick_v, take_v, give_v, got_v),
    ):
        to_twin(a, stage, held).wait_send()
        others(n, first, lambda p: out_first(a, held, p).wait_send())
        others(n, second, lambda q: out_second(a, pick, take, q).wait_send())
        other_half(a, give, got).wait_send()
    others(members, mine, lambda m: f1(m).wait_send())
    others(n, zz, lambda z: f2(z).wait_send())
    others(members, mine, lambda m: f4(m).wait_send())
    others(nx, here, lambda s: f5(s).wait_send())


def solution(mesh):
    walkers = mesh.shape["walker"]
    nx = mesh.shape["space"]
    n = 1
    while 2 * n * n < walkers:
        n += 1
    members = 2 * n

    def shards(positions, velocities, weights, strength, tiles, plan, home):
        cells = tiles.shape[0]
        ext = cells + 2 * HALO
        f32 = jnp.float32
        vmem = pl.BlockSpec(memory_space=pltpu.VMEM)
        smem = pl.BlockSpec(memory_space=pltpu.SMEM)
        dma = pltpu.SemaphoreType.DMA
        sites = members * TILE * nx
        block = jax.ShapeDtypeStruct((3, cells, TILE), f32)
        dist, npos, nvel, nwt = pl.pallas_call(
            functools.partial(kernel, n, nx, sites),
            out_shape=(
                jax.ShapeDtypeStruct((1, walkers // nx), f32),
                block,
                block,
                jax.ShapeDtypeStruct((1, 1), f32),
            ),
            in_specs=[vmem] * 5 + [smem] * 3,
            out_specs=(vmem,) * 4,
            scratch_shapes=[
                pltpu.VMEM((3, ext, TILE, TILE), f32),
                pltpu.VMEM((3, ext, TILE, TILE), f32),
                pltpu.VMEM((ext, TILE, TILE), f32),
                pltpu.VMEM((REACH, cells, TILE), f32),
                pltpu.VMEM((3, cells, TILE), f32),
                pltpu.VMEM((3, cells, TILE), f32),
                pltpu.VMEM((3, 8, TILE), f32),
                pltpu.VMEM((3, 8, TILE), f32),
                pltpu.VMEM((8, TILE), f32),
                pltpu.VMEM((8, TILE), f32),
                pltpu.VMEM((3, 8, TILE), f32),
                pltpu.VMEM((3, 8, TILE), f32),
                pltpu.VMEM((2, ROWS, TILE), f32),
                pltpu.VMEM((2, ROWS, TILE), f32),
                pltpu.VMEM((members, 8, TILE), f32),
                pltpu.VMEM((members, 8, TILE), f32),
                pltpu.VMEM((n, members, 3 * TILE), jnp.bfloat16),
                pltpu.VMEM((walkers, 3 * TILE), f32),
                pltpu.VMEM((3, members, TILE), f32),
                pltpu.VMEM((members, 8, TILE), f32),
                pltpu.VMEM((members, 8, TILE), f32),
                pltpu.VMEM((nx, 8, TILE), f32),
                pltpu.VMEM((members, ROWS, TILE), f32),
                pltpu.VMEM((members, ROWS, TILE), f32),
                pltpu.VMEM((n, 2, ROWS, TILE), f32),
                pltpu.VMEM((n, 2, ROWS, TILE), f32),
                pltpu.VMEM((n, 2, ROWS, TILE), f32),
                pltpu.VMEM((n, 2, ROWS, TILE), f32),
                pltpu.VMEM((ROWS, TILE), f32),
                pltpu.VMEM((ROWS, TILE), f32),
                pltpu.VMEM((ROWS, TILE), f32),
                pltpu.VMEM((ROWS, TILE), f32),
                dma((6,)),
                dma((6,)),
                dma((members,)),
                dma((members,)),
                dma((n,)),
                dma((n,)),
                dma((members,)),
                dma((members,)),
                dma((nx,)),
                dma((nx,)),
                dma((2,)),
                dma((2,)),
                dma((2 * n,)),
                dma((2 * n,)),
                dma((2 * n,)),
                dma((2 * n,)),
                dma((2,)),
                dma((2,)),
            ],
            compiler_params=pltpu.CompilerParams(
                collective_id=0,
                has_side_effects=True,
                vmem_limit_bytes=40 * 1024 * 1024,
            ),
        )(
            positions.reshape(3, cells, TILE),
            velocities.reshape(3, cells, TILE),
            strength.reshape(cells, TILE),
            tiles,
            plan.reshape(1, walkers),
            weights,
            plan,
            home,
        )
        return (
            dist,
            npos.reshape(1, 3, cells * TILE),
            nvel.reshape(1, 3, cells * TILE),
            nwt.reshape(1),
        )

    return jax.shard_map(
        shards,
        mesh=mesh,
        in_specs=(
            P("walker", None, "space"),
            P("walker", None, "space"),
            P("walker"),
            P("space"),
            P("space", None),
            P(),
            P(),
        ),
        out_specs=(
            P("walker", "space"),
            P("walker", None, "space"),
            P("walker", None, "space"),
            P("walker"),
        ),
        check_vma=False,
    )
```

time: 730 us -> 67.4 us (0.09)
  other arithmetic: 283 us -> 0 us
  blocking collectives: 247 us -> 0 us
  waiting for transfers between devices: 94.6 us -> 0 us
  local copies, waits for them, and re-layouts: 71.6 us -> 5.35 us
  Pallas kernels: 0 us -> 58.6 us
  between operations: 17.1 us -> 3.13 us
  starting transfers between devices: 9.8 us -> 0 us
    reduce_sum x114 -> x0, other arithmetic: 251 us -> none  [the longest x54 155 us: tile_force(): return jnp.sum(factor[:, None] * delta, axis=-1)]
    unnamed x1 -> x0, blocking collectives: 247 us -> none
    all_gather x3 -> x0, waiting for transfers between devices: 90 us -> none  [the longest x1 90 us: shards(): lax.all_gather(own_features[None], 'walker', axis=0, tiled=True)]
    gather x108 -> x0, local copies, waits for them, and re-layouts: 62.8 us -> none  [the longest x54 32.2 us: turn(): near = jnp.take(ext_pos, column, axis=2)]
    pallas_call x0 -> x1, Pallas kernels: none -> 58.6 us  [shards(): pl.pallas_call(functools.partial(kernel, n, nx, sites), out_shape=(jax.Sh...]
    div x55 -> x0, other arithmetic: 13.2 us -> none  [the longest x54 12.7 us: tile_force(): factor = near_str[:, None, :] / jnp.square(1.0 + radius)]
    ppermute x4 -> x0, starting transfers between devices: 9.64 us -> none  [the longest x2 7.05 us: with_halo(): lax.ppermute(lax.slice_in_dim(block, block.shape[dim] - width, None, axis...]
  transfers between devices with their start and end apart: 8 -> 0, of which waited for: 3 -> 0; matrix products, arithmetic and copies ran while one was open for 1% -> 0% of each run, Pallas kernels for 0% -> 0%
where the time goes in v1:
time: 67.4 us; the launch traced here: 67 us
  Pallas kernels  58.6 us (87%)
  local copies, waits for them, and re-layouts  5.35 us (8%)
  between operations  3.13 us (5%)
    pallas_call x1, Pallas kernels, shards(): pl.pallas_call(functools.partial(kernel, n, nx, sites), out_shape=(jax.Sh...  58.6 us
    unnamed x15, local copies, waits for them, and re-layouts  5.35 us

profile of v1, /device:TPU:1, one launch (start us, length us, event | category | flops | bytes accessed | tf_op | source)
XLA Modules:
  0.0 67.0 jit_solution(15058097031924469311)
XLA Ops:
  1.3 0.0 copy-start.4
  1.3 0.0 copy-start.5
  1.3 0.6 copy-done.4
  1.9 0.0 copy-done.5
  1.9 0.0 copy-start
  2.0 0.8 %copy-done = f32[1,3,3072]{2,0,1:T(1,128)S(1)} copy-done((f32[1,3,3072]{2,0,1:T(1,128)S(1)}, f32[1,3,3072]{2,0,1:T(1,128)}, u32[]{:S(2)}) %copy-start) | copy-done | bytes 36888
  2.7 0.0 copy-start.1
  2.7 0.8 %copy-done.1 = f32[1,3,3072]{2,0,1:T(1,128)S(1)} copy-done((f32[1,3,3072]{2,0,1:T(1,128)S(1)}, f32[1,3,3072]{2,0,1:T(1,128)}, u32[]{:S(2)}) %copy-start.1) | copy-done | bytes 36888
  3.5 0.0 copy-start.2
  3.5 0.7 %copy-done.2 = f32[3072]{0:T(1024)S(1)} copy-done((f32[3072]{0:T(1024)S(1)}, f32[3072]{0:T(1024)}, u32[]{:S(2)}) %copy-start.2) | copy-done | bytes 12312
  4.2 0.0 copy-start.3
  4.2 0.7 %copy-done.3 = s32[24,27]{1,0:T(8,128)S(1)} copy-done((s32[24,27]{1,0:T(8,128)S(1)}, s32[24,27]{1,0:T(8,128)}, u32[]{:S(2)}) %copy-start.3) | copy-done | bytes 2616
  4.9 58.6 %shard_map.102 = (f32[1,32]{1,0:T(1,128)S(1)}, f32[3,24,128]{2,1,0:T(8,128)S(1)}, f32[3,24,128]{2,1,0:T(8,128)S(1)}, f32[1,1]{1,0:T(1,128)}) custom-call(f32[3,24,128]{2,1,0:T(8,128)S(1)} %bitcast.7, f32[3,24,128]{2,1,0:T(8,128)S(1)} %bitcast.8, f32[24,128]{1,0:T(8,128)S(1)} %bitcast.11, s32[24,27]{1,0:T(8,128)S(1)} %copy-done.3, s32[1,128]{1,0:T(1,128)S(1)} %bitcast.12, ...), custom_call_target="tpu_custom_call" | custom-call | tf_op jit(solution)/shard_map/pallas_call | solution.py:530
  63.5 0.5 copy.20
  64.0 0.6 copy.21
  64.6 0.6 copy.22
Async XLA Ops:
  1.3 0.7 copy-start.4
  1.3 0.7 copy-start.5
  1.9 0.8 %copy-start = (f32[1,3,3072]{2,0,1:T(1,128)S(1)}, f32[1,3,3072]{2,0,1:T(1,128)}, u32[]{:S(2)}) copy-start(f32[1,3,3072]{2,0,1:T(1,128)} %param.7) | copy-start | bytes 110596
  2.7 0.8 %copy-start.1 = (f32[1,3,3072]{2,0,1:T(1,128)S(1)}, f32[1,3,3072]{2,0,1:T(1,128)}, u32[]{:S(2)}) copy-start(f32[1,3,3072]{2,0,1:T(1,128)} %param.8) | copy-start | bytes 110596
  3.5 0.7 %copy-start.2 = (f32[3072]{0:T(1024)S(1)}, f32[3072]{0:T(1024)}, u32[]{:S(2)}) copy-start(f32[3072]{0:T(1024)} %param.10) | copy-start | bytes 36868
  4.2 0.7 %copy-start.3 = (s32[24,27]{1,0:T(8,128)S(1)}, s32[24,27]{1,0:T(8,128)}, u32[]{:S(2)}) copy-start(s32[24,27]{1,0:T(8,128)} %til.1) | copy-start | bytes 7780

commit v2 on v0

v2 whole, which is shorter than its diff:
```python
import functools

import jax
import jax.numpy as jnp
from jax import lax
from jax.experimental import pallas as pl
from jax.experimental.pallas import tpu as pltpu
from jax.sharding import PartitionSpec as P

HALO = 2
REACH = 2 * HALO + 1
STEP = 0.1
TILE = 128
ROWS = 40
SPLIT = 24
KEYS = 48
CHUNK = 64
MESH = pl.DeviceIdType.MESH


def kernel(
    n,
    nx,
    pos_in,
    vel_in,
    stg_in,
    til_in,
    row_in,
    plan_in,
    home_in,
    wgt,
    dist,
    npos,
    nvel,
    nwt,
    pos,
    vel,
    stg,
    til,
    planv,
    plan,
    home,
    side_j,
    next_j,
    side_i,
    next_i,
    base_w,
    next_w,
    mult,
    x1,
    v1,
    low_p,
    high_p,
    low_s,
    high_s,
    low_n,
    high_n,
    stage_x,
    stage_va,
    stage_vb,
    feat,
    feat_in,
    group,
    wide,
    own_rows,
    part,
    part_in,
    line,
    held_x,
    held_va,
    held_vb,
    pick_x,
    pick_va,
    pick_vb,
    take_x,
    take_va,
    take_vb,
    load_sem,
    halo_send,
    halo_recv,
    feat_send,
    feat_recv,
    one_send,
    one_recv,
    two_send,
    two_recv,
):
    cells = pos.shape[1]
    members = 2 * n
    walkers = members * n
    near = cells - 8
    sites = members * TILE * nx
    me = lax.axis_index("walker")
    here = lax.axis_index("space")
    core = me % 2
    yy = (me // 2) % n
    zz = me // members
    mine = me % members

    first = zz + core * (yy - zz)
    second = yy + core * (zz - yy)
    first_stride = 2 * (n - (n - 1) * core)
    second_stride = 2 * (1 + (n - 1) * core)
    pair = 1 - core
    twin = me + pair - core

    loads = [
        pltpu.make_async_copy(src, dst, load_sem.at[i])
        for i, (src, dst) in enumerate(
            ((pos_in, pos), (stg_in, stg), (til_in, til), (vel_in, vel), (row_in, planv), (plan_in, plan), (home_in, home))
        )
    ]
    for copy in loads:
        copy.start()

    def member(m):
        return (zz * members + m, here)

    def level(z):
        return (z * members + mine, here)

    right = (me, (here + 1) % nx)
    left = (me, (here + nx - 1) % nx)

    def others(count, own, act):
        def body(k, _):
            act((own + k) % count)
            return 0

        lax.fori_loop(1, count, body, 0)

    barrier = pltpu.get_barrier_semaphore()

    def hello(where):
        pl.semaphore_signal(barrier, inc=1, device_id=where, device_id_type=MESH)

    others(nx, here, lambda s: hello((me, s)))
    others(members, mine, lambda m: hello(member(m)))

    def hello_level(z):
        hello(level(z))
        hello((z * members + mine + pair - core, here))

    others(n, zz, hello_level)

    def remote(src, dst, send, recv, where):
        return pltpu.make_async_remote_copy(
            src_ref=src,
            dst_ref=dst,
            send_sem=send,
            recv_sem=recv,
            device_id=where,
            device_id_type=MESH,
        )

    def wait_all(ref, sem):
        pltpu.make_async_copy(ref, ref, sem).wait()

    for h in range(2):
        stage_x[h, pl.ds(36, 4), :] = jnp.broadcast_to(wgt[0], (4, TILE))
        stage_vb[h, pl.ds(12, 4), :] = jnp.zeros((4, TILE), jnp.float32)
    feat[...] = jnp.zeros(feat.shape, jnp.float32)
    x1[...] = jnp.zeros(x1.shape, jnp.float32)

    for copy in loads[:3]:
        copy.wait()

    shift = til[...] - lax.broadcasted_iota(jnp.int32, til.shape, 0)
    hits = [
        jnp.broadcast_to(
            jnp.sum((shift == o).astype(jnp.float32), axis=1, keepdims=True), (cells, TILE)
        )
        for o in range(REACH)
    ]
    none = jnp.zeros((4, TILE), jnp.float32)
    for k in range(REACH + 1):
        for p in range(cells // 2):
            for row, g, o in ((0, 2 * p, k), (4, 2 * p + 1, k - 1)):
                value = none
                if 0 <= o < REACH:
                    value = jnp.broadcast_to(hits[o][g : g + 1], (4, TILE))
                mult[k, p, row : row + 4, :] = value

    def thirds(x):
        high = x.astype(jnp.bfloat16).astype(jnp.float32)
        rest = x - high
        middle = rest.astype(jnp.bfloat16).astype(jnp.float32)
        return high, middle, rest - middle

    one_row = jnp.ones((1, TILE), jnp.float32)
    three_rows = jnp.zeros((3, TILE), jnp.float32)

    def prepare(to_j, to_w, cell, x, s, to_i=None):
        norm = x[0] * x[0] + x[1] * x[1] + x[2] * x[2]
        a, b, c = thirds(
            jnp.concatenate([x[0], x[1], x[2], norm + 1.0, one_row, three_rows], axis=0)
        )
        keys = jnp.concatenate([a, a, b, b, a, c], axis=0).T
        to_j[pl.ds(pl.multiple_of(cell * TILE, TILE), TILE), :] = keys.astype(jnp.bfloat16)
        four = [s, s * x[0], s * x[1], s * x[2]]
        to_w[cell] = jnp.concatenate(four + four, axis=0)
        if to_i is not None:
            a, b, c = thirds(
                jnp.concatenate(
                    [-2.0 * x[0], -2.0 * x[1], -2.0 * x[2], one_row, norm, three_rows], axis=0
                )
            )
            ref, p, lane = to_i
            ref[p, :, TILE * lane : TILE * (lane + 1)] = jnp.concatenate(
                [a, b, a, b, c, a], axis=0
            ).astype(jnp.bfloat16)

    def prepare_pair(source, to_j, to_w, to_i, p):
        for lane in range(2):
            g = 2 * p + lane
            prepare(
                to_j,
                to_w,
                g + HALO,
                [source[d, pl.ds(g, 1), :] for d in range(3)],
                stg[pl.ds(g, 1), :],
                (to_i, p, lane),
            )

    def prepare_own(p, _):
        prepare_pair(pos, side_j, base_w, side_i, p)
        return 0

    lax.fori_loop(0, cells // 2, prepare_own, 0)
    for copy in loads[3:]:
        copy.wait()

    def prepare_halo(to_j, to_w, low, high):
        for k in range(HALO):
            for base, at, pos_of, str_of in (
                (0, 8 - HALO, low, low_s),
                (HALO + cells, 0, high, high_s),
            ):
                prepare(
                    to_j,
                    to_w,
                    base + k,
                    [pos_of[d, at + k : at + k + 1, :] for d in range(3)],
                    str_of[at + k : at + k + 1, :],
                )

    def force(of_j, of_i, of_w, source, p):
        weights = []
        for k in range(REACH + 1):
            parts = thirds(mult[k, p] * of_w[2 * p + k])
            weights.append(
                jnp.concatenate(list(parts) + [jnp.zeros((8, TILE), jnp.float32)], axis=0)
            )
        weights = jnp.concatenate(weights, axis=1).astype(jnp.bfloat16)
        keys_i = of_i[p]
        total = None
        for k in range((REACH + 1) // 2):
            highs, lows = [], []
            for b in range(2 * TILE // CHUNK):
                at = pl.multiple_of(p * 2 * TILE, 2 * TILE) + k * 2 * TILE + b * CHUNK
                q = jnp.dot(
                    of_j[pl.ds(at, CHUNK), :], keys_i, preferred_element_type=jnp.float32
                )
                f = pltpu.reciprocal(q * q, approx=True)
                high = f.astype(jnp.bfloat16)
                highs.append(high)
                lows.append((f - high.astype(jnp.float32)).astype(jnp.bfloat16))
            w = weights[:, 2 * TILE * k : 2 * TILE * (k + 1)]
            for piece in (highs, lows):
                term = jnp.dot(
                    w, jnp.concatenate(piece, axis=0), preferred_element_type=jnp.float32
                )
                total = term if total is None else total + term
        total = total[0:8] + (total[8:16] + total[16:24])
        result = []
        for lane in range(2):
            g = 2 * p + lane
            part_of = total[4 * lane : 4 * lane + 4, TILE * lane : TILE * (lane + 1)]
            s = stg[pl.ds(g, 1), :]
            result.append(
                [
                    s * (source[d, pl.ds(g, 1), :] * part_of[0:1] - part_of[d + 1 : d + 2])
                    for d in range(3)
                ]
            )
        return result

    def stage_at(g):
        inner = g < near
        h = jnp.where(inner, g // 8, (g - near) // 4)
        base = jnp.where(inner, g % 8, SPLIT + (g - near) % 4)
        return h, base, jnp.where(inner, 8, 4)

    top = cells - 8
    halos = [
        remote(pos.at[:, pl.ds(top, 8), :], low_p, halo_send.at[0], halo_recv.at[0], right),
        remote(pos.at[:, pl.ds(0, 8), :], high_p, halo_send.at[1], halo_recv.at[1], left),
        remote(stg.at[pl.ds(top, 8), :], low_s, halo_send.at[2], halo_recv.at[2], right),
        remote(stg.at[pl.ds(0, 8), :], high_s, halo_send.at[3], halo_recv.at[3], left),
    ]
    nexts = [
        remote(x1.at[:, pl.ds(top, 8), :], low_n, halo_send.at[4], halo_recv.at[4], right),
        remote(x1.at[:, pl.ds(0, 8), :], high_n, halo_send.at[5], halo_recv.at[5], left),
    ]

    pairs = cells // 2

    def order_one(t):
        return (t + 1) % pairs

    def first_step(t, _):
        @pl.when(t == 2)
        def _():
            pl.semaphore_wait(barrier, (nx - 1) + (members - 1) + 2 * (n - 1))
            for copy in halos:
                copy.start()

        @pl.when(t == pairs - 2)
        def _():
            for copy in halos:
                copy.wait()
            prepare_halo(side_j, base_w, low_p, high_p)

        p = order_one(t)
        prepare_pair(x1, next_j, next_w, next_i, order_one(t + pairs - 1))
        f = force(side_j, side_i, base_w, pos, p)
        for lane in range(2):
            g = 2 * p + lane
            h, base, stride = stage_at(g)
            for d in range(3):
                v = vel[d, pl.ds(g, 1), :] + STEP * f[lane][d]
                x = pos[d, pl.ds(g, 1), :] + STEP * v
                v1[d, pl.ds(g, 1), :] = v
                x1[d, pl.ds(g, 1), :] = x
                stage_x[h, pl.ds(base + d * stride, 1), :] = x
        return 0

    lax.fori_loop(0, pairs, first_step, 0)
    for copy in nexts:
        copy.start()

    def spread_state(a, stage, held):
        for h, own, low, step in ((0, zz, 2 * yy, members), (1, yy, zz * members + 1, 2)):

            def send(p, h=h, own=own, low=low, step=step):
                remote(
                    stage.at[h],
                    held.at[2 * own + core],
                    one_send.at[a],
                    one_recv.at[a],
                    (low + p * step, here),
                ).start()

            others(n, own, send)
        remote(
            stage.at[pair],
            held.at[2 * second + core],
            one_send.at[a],
            one_recv.at[a],
            (twin, here),
        ).start()
        held[2 * first + core] = stage[core]

    def source_of(slot):
        row = home[plan[slot]]
        return row // members, (row // 2) % n, row % 2

    def hand_on(a, held, pick, take):
        wait_all(held.at[pl.ds(0, members - 1)], one_recv.at[a])

        def choose(q, _):
            for c in range(2):
                slot = first * first_stride + q * second_stride + c
                z, y, c_src = source_of(slot)
                p = z + core * (y - z)
                pick[2 * q + c] = held[2 * p + c_src]

                @pl.when(slot != me)
                def _(slot=slot, c=c):
                    remote(
                        pick.at[2 * q + c],
                        take.at[core * n + second],
                        two_send.at[a],
                        two_recv.at[a],
                        (slot, here),
                    ).start()

            return 0

        lax.fori_loop(0, n, choose, 0)
        take[core * n + second] = pick[2 * second + core]

    spread_state(0, stage_x, held_x)
    prepare_pair(x1, next_j, next_w, next_i, order_one(pairs - 1))

    def share_features():
        feat_in[mine] = feat[mine]
        wait_all(feat_in.at[pl.ds(0, members - 1)], feat_recv.at[0])
        for d in range(3):
            group[zz, :, TILE * d : TILE * (d + 1)] = feat_in[:, d, :].astype(jnp.bfloat16)
        others(
            n,
            zz,
            lambda z: remote(
                group.at[zz], group.at[zz], feat_send.at[1], feat_recv.at[1], level(z)
            ).start(),
        )

    near_pairs = near // 2

    def second_step(t, _):
        @pl.when(t == near_pairs - 1)
        def _():
            for copy in nexts:
                copy.wait()
            prepare_halo(next_j, next_w, low_n, high_n)

        @pl.when(t == near_pairs)
        def _():
            spread_state(1, stage_va, held_va)

        @pl.when(t == near_pairs + 1)
        def _():
            share_features()
            hand_on(0, held_x, pick_x, take_x)

        p = jnp.where(t < near_pairs, (t + 1) % near_pairs, t)
        f = force(next_j, next_i, next_w, x1, p)
        for lane in range(2):
            g = 2 * p + lane
            h, base, stride = stage_at(g)
            for d in range(3):
                v = v1[d, pl.ds(g, 1), :] + STEP * f[lane][d]
                x = x1[d, pl.ds(g, 1), :] + STEP * v

                @pl.when(t < near_pairs)
                def _(v=v, h=h, base=base, d=d):
                    stage_va[h, pl.ds(base + 8 * d, 1), :] = v

                @pl.when(t >= near_pairs)
                def _(v=v, h=h, base=base, d=d):
                    stage_vb[h, pl.ds(base - SPLIT + 4 * d, 1), :] = v

                feat[g, pl.ds(d, 1), :] = x

            @pl.when((g < members) & (g != mine))
            def _(g=g):
                remote(
                    feat.at[g], feat_in.at[mine], feat_send.at[0], feat_recv.at[0], member(g)
                ).start()

        return 0

    lax.fori_loop(0, pairs, second_step, 0)
    spread_state(2, stage_vb, held_vb)
    hand_on(1, held_va, pick_va, take_va)

    wait_all(group.at[pl.ds(0, n - 1)], feat_recv.at[1])
    wide[...] = group[...].astype(jnp.float32).reshape(walkers, 3 * TILE)
    for d in range(3):
        own_rows[d] = group[zz, :, TILE * d : TILE * (d + 1)].astype(jnp.float32)
    lanes = lax.broadcasted_iota(jnp.int32, (walkers, TILE), 1)

    def row_of(r, acc):
        total = None
        for d in range(3):
            diff = wide[:, TILE * d : TILE * (d + 1)] - own_rows[d, pl.ds(r, 1), :]
            square = diff * diff
            total = square if total is None else total + square
        return jnp.where(lanes == r, jnp.sum(total, axis=1, keepdims=True), acc)

    sums = lax.fori_loop(0, members, row_of, jnp.zeros((walkers, TILE), jnp.float32)).T
    for r in range(members):
        part[r, :, 0:walkers] = jnp.broadcast_to(sums[r : r + 1], (8, walkers))
    others(
        members,
        mine,
        lambda m: remote(
            part.at[m], part_in.at[mine], feat_send.at[2], feat_recv.at[2], member(m)
        ).start(),
    )
    part_in[mine] = part[mine]

    hand_on(2, held_vb, pick_vb, take_vb)

    wait_all(part_in.at[pl.ds(0, members - 1)], feat_recv.at[2])
    row = part_in[0]
    for m in range(1, members):
        row = row + part_in[m]
    line[here] = row
    others(
        nx,
        here,
        lambda s: remote(
            line.at[here], line.at[here], feat_send.at[3], feat_recv.at[3], (me, s)
        ).start(),
    )
    wait_all(line.at[pl.ds(0, nx - 1)], feat_recv.at[3])
    row = line[0, 0:1, 0:walkers]
    for s in range(1, nx):
        row = row + line[s, 0:1, 0:walkers]
    row = row / (3.0 * sites)
    share = walkers // nx
    mine_of = row[:, 0:share]
    for s in range(1, nx):
        mine_of = jnp.where(here == s, row[:, share * s : share * (s + 1)], mine_of)
    dist[...] = mine_of

    for a, take in enumerate((take_x, take_va, take_vb)):
        wait_all(take.at[pl.ds(0, members - 1)], two_recv.at[a])

    z, y, _ = source_of(me)
    for h, index in ((0, y), (1, n + z)):
        x = take_x[index]
        va = take_va[index]
        vb = take_vb[index]
        if h == 0:
            same = (planv[...] == plan[me]).astype(jnp.float32)
            nwt[...] = x[36:37, 0:1] / jnp.sum(same, axis=1, keepdims=True)
        xa = x[0:SPLIT] + STEP * va
        xb = x[SPLIT:ROWS] + STEP * vb
        for out, of_a, of_b in ((nvel, va, vb), (npos, xa, xb)):
            for d in range(3):
                out[d, 8 * h : 8 * h + 8, :] = of_a[8 * d : 8 * d + 8]
                out[d, near + 4 * h : near + 4 * h + 4, :] = of_b[4 * d : 4 * d + 4]

    for a, held in enumerate((held_x, held_va, held_vb)):
        wait_all(held.at[pl.ds(0, members - 1)], one_send.at[a])
        wait_all(held.at[pl.ds(0, members - 1)], two_send.at[a])
    wait_all(feat_in.at[pl.ds(0, members - 1)], feat_send.at[0])
    wait_all(group.at[pl.ds(0, n - 1)], feat_send.at[1])
    wait_all(part_in.at[pl.ds(0, members - 1)], feat_send.at[2])
    wait_all(line.at[pl.ds(0, nx - 1)], feat_send.at[3])


def solution(mesh):
    walkers = mesh.shape["walker"]
    nx = mesh.shape["space"]
    n = 1
    while 2 * n * n < walkers:
        n += 1
    members = 2 * n

    def shards(positions, velocities, weights, strength, tiles, plan, home):
        cells = tiles.shape[0]
        ext = cells + 2 * HALO
        f32 = jnp.float32
        vmem = pl.BlockSpec(memory_space=pltpu.VMEM)
        smem = pl.BlockSpec(memory_space=pltpu.SMEM)
        hbm = pl.BlockSpec(memory_space=pltpu.HBM)
        dma = pltpu.SemaphoreType.DMA
        block = jax.ShapeDtypeStruct((3, cells, TILE), f32)

        def pinned(x):
            return pltpu.with_memory_space_constraint(x, pltpu.HBM)

        def room(*shape, kind=f32):
            return pltpu.VMEM(shape, kind)

        dist, npos, nvel, nwt = pl.pallas_call(
            functools.partial(kernel, n, nx),
            out_shape=(
                jax.ShapeDtypeStruct((1, walkers // nx), f32),
                block,
                block,
                jax.ShapeDtypeStruct((1, 1), f32),
            ),
            in_specs=[hbm] * 7 + [smem],
            out_specs=(vmem,) * 4,
            scratch_shapes=[
                room(3, cells, TILE),
                room(3, cells, TILE),
                room(cells, TILE),
                room(*tiles.shape, kind=jnp.int32),
                room(1, walkers, kind=jnp.int32),
                pltpu.SMEM((walkers,), jnp.int32),
                pltpu.SMEM((walkers,), jnp.int32),
                room(ext * TILE, KEYS, kind=jnp.bfloat16),
                room(ext * TILE, KEYS, kind=jnp.bfloat16),
                room(cells // 2, KEYS, 2 * TILE, kind=jnp.bfloat16),
                room(cells // 2, KEYS, 2 * TILE, kind=jnp.bfloat16),
                room(ext, 8, TILE),
                room(ext, 8, TILE),
                room(REACH + 1, cells // 2, 8, TILE),
                room(3, cells, TILE),
                room(3, cells, TILE),
                room(3, 8, TILE),
                room(3, 8, TILE),
                room(8, TILE),
                room(8, TILE),
                room(3, 8, TILE),
                room(3, 8, TILE),
                room(2, ROWS, TILE),
                room(2, SPLIT, TILE),
                room(2, ROWS - SPLIT, TILE),
                room(cells, 8, TILE),
                room(members, 8, TILE),
                room(n, members, 3 * TILE, kind=jnp.bfloat16),
                room(walkers, 3 * TILE),
                room(3, members, TILE),
                room(members, 8, TILE),
                room(members, 8, TILE),
                room(nx, 8, TILE),
                room(members, ROWS, TILE),
                room(members, SPLIT, TILE),
                room(members, ROWS - SPLIT, TILE),
                room(members, ROWS, TILE),
                room(members, SPLIT, TILE),
                room(members, ROWS - SPLIT, TILE),
                room(members, ROWS, TILE),
                room(members, SPLIT, TILE),
                room(members, ROWS - SPLIT, TILE),
                dma((7,)),
                dma((6,)),
                dma((6,)),
                dma((4,)),
                dma((4,)),
                dma((3,)),
                dma((3,)),
                dma((3,)),
                dma((3,)),
            ],
            compiler_params=pltpu.CompilerParams(
                collective_id=0,
                has_side_effects=True,
                vmem_limit_bytes=40 * 1024 * 1024,
            ),
        )(
            pinned(positions.reshape(3, cells, TILE)),
            pinned(velocities.reshape(3, cells, TILE)),
            pinned(strength.reshape(cells, TILE)),
            pinned(tiles),
            pinned(plan.reshape(1, walkers)),
            pinned(plan),
            pinned(home),
            weights,
        )
        return (
            dist,
            npos.reshape(1, 3, cells * TILE),
            nvel.reshape(1, 3, cells * TILE),
            nwt.reshape(1),
        )

    return jax.shard_map(
        shards,
        mesh=mesh,
        in_specs=(
            P("walker", None, "space"),
            P("walker", None, "space"),
            P("walker"),
            P("space"),
            P("space", None),
            P(),
            P(),
        ),
        out_specs=(
            P("walker", "space"),
            P("walker", None, "space"),
            P("walker", None, "space"),
            P("walker"),
        ),
        check_vma=False,
    )
```

time: 730 us -> 52.9 us (0.07)
  other arithmetic: 283 us -> 0 us
  blocking collectives: 247 us -> 0 us
  waiting for transfers between devices: 94.6 us -> 0 us
  local copies, waits for them, and re-layouts: 71.6 us -> 1.74 us
  Pallas kernels: 0 us -> 47.9 us
  between operations: 17.1 us -> 2.98 us
  starting transfers between devices: 9.8 us -> 0 us
    reduce_sum x114 -> x0, other arithmetic: 251 us -> none  [the longest x54 155 us: tile_force(): return jnp.sum(factor[:, None] * delta, axis=-1)]
    unnamed x1 -> x0, blocking collectives: 247 us -> none
    all_gather x3 -> x0, waiting for transfers between devices: 90 us -> none  [the longest x1 90 us: shards(): lax.all_gather(own_features[None], 'walker', axis=0, tiled=True)]
    gather x108 -> x0, local copies, waits for them, and re-layouts: 62.8 us -> none  [the longest x54 32.2 us: turn(): near = jnp.take(ext_pos, column, axis=2)]
    pallas_call x0 -> x1, Pallas kernels: none -> 47.9 us  [shards(): pl.pallas_call(functools.partial(kernel, n, nx), out_shape=(jax.ShapeDtyp...]
    div x55 -> x0, other arithmetic: 13.2 us -> none  [the longest x54 12.7 us: tile_force(): factor = near_str[:, None, :] / jnp.square(1.0 + radius)]
    ppermute x4 -> x0, starting transfers between devices: 9.64 us -> none  [the longest x2 7.05 us: with_halo(): lax.ppermute(lax.slice_in_dim(block, block.shape[dim] - width, None, axis...]
  transfers between devices with their start and end apart: 8 -> 0, of which waited for: 3 -> 0; matrix products, arithmetic and copies ran while one was open for 1% -> 0% of each run, Pallas kernels for 0% -> 0%
where the time goes in v2:
time: 52.9 us; the launch traced here: 52.6 us
  Pallas kernels  47.9 us (91%)
  between operations  2.98 us (6%)
  local copies, waits for them, and re-layouts  1.74 us (3%)
    pallas_call x1, Pallas kernels, shards(): pl.pallas_call(functools.partial(kernel, n, nx), out_shape=(jax.ShapeDtyp...  47.9 us
    unnamed x3, local copies, waits for them, and re-layouts  1.74 us

profile of v2, /device:TPU:1, one launch (start us, length us, event | category | flops | bytes accessed | tf_op | source)
XLA Modules:
  0.0 52.6 jit_solution(11405230898156661827)
XLA Ops:
  1.3 47.9 %shard_map.102 = (f32[1,32]{1,0:T(1,128)S(1)}, f32[3,24,128]{2,1,0:T(8,128)S(1)}, f32[3,24,128]{2,1,0:T(8,128)S(1)}, f32[1,1]{1,0:T(1,128)}) custom-call(f32[3,24,128]{2,1,0:T(8,128)} %bitcast.9, f32[3,24,128]{2,1,0:T(8,128)} %bitcast.10, f32[24,128]{1,0:T(8,128)} %bitcast.11, s32[24,27]{1,0:T(8,128)} %til_in.1, s32[1,128]{1,0:T(1,128)} %bitcast.12, ...), custom_call_target="tpu_custom_call" | custom-call | tf_op jit(solution)/shard_map/pallas_call | solution.py:560
  49.2 0.5 copy.20
  49.7 0.6 %copy.21 = f32[1,3,3072]{2,0,1:T(1,128)} copy(f32[1,3,3072]{2,0,1:T(1,128)S(1)} %bitcast.8) | data formatting | bytes 73728
  50.3 0.6 %copy.22 = f32[1,3,3072]{2,0,1:T(1,128)} copy(f32[1,3,3072]{2,0,1:T(1,128)S(1)} %bitcast.7) | data formatting | bytes 73728

commit v3 on v2

--- a/solution.py
+++ b/solution.py
@@ -14,7 +14,7 @@
 ROWS = 40
 SPLIT = 24
 KEYS = 48
-CHUNK = 64
+CHUNK = 32
 MESH = pl.DeviceIdType.MESH
 
 
@@ -123,11 +123,8 @@
     left = (me, (here + nx - 1) % nx)
 
     def others(count, own, act):
-        def body(k, _):
-            act((own + k) % count)
-            return 0
-
-        lax.fori_loop(1, count, body, 0)
+        for k in range(1, count):
+            act(lax.rem(own + k, count))
 
     barrier = pltpu.get_barrier_semaphore()
 
@@ -256,11 +253,12 @@
         total = None
         for k in range((REACH + 1) // 2):
             highs, lows = [], []
+            at = pl.multiple_of((p + k) * 2 * TILE, 2 * TILE)
+            block = jnp.dot(
+                of_j[pl.ds(at, 2 * TILE), :], keys_i, preferred_element_type=jnp.float32
+            )
             for b in range(2 * TILE // CHUNK):
-                at = pl.multiple_of(p * 2 * TILE, 2 * TILE) + k * 2 * TILE + b * CHUNK
-                q = jnp.dot(
-                    of_j[pl.ds(at, CHUNK), :], keys_i, preferred_element_type=jnp.float32
-                )
+                q = block[CHUNK * b : CHUNK * (b + 1)]
                 f = pltpu.reciprocal(q * q, approx=True)
                 high = f.astype(jnp.bfloat16)
                 highs.append(high)
@@ -363,31 +361,32 @@
 
     def source_of(slot):
         row = home[plan[slot]]
-        return row // members, (row // 2) % n, row % 2
+        return lax.div(row, members), lax.rem(lax.div(row, 2), n), lax.rem(row, 2)
+
+    slots, origins = [], []
+    for q in range(n):
+        for c in range(2):
+            slot = first * first_stride + q * second_stride + c
+            z, y, c_src = source_of(slot)
+            slots.append(slot)
+            origins.append(2 * (z + core * (y - z)) + c_src)
 
     def hand_on(a, held, pick, take):
         wait_all(held.at[pl.ds(0, members - 1)], one_recv.at[a])
 
-        def choose(q, _):
-            for c in range(2):
-                slot = first * first_stride + q * second_stride + c
-                z, y, c_src = source_of(slot)
-                p = z + core * (y - z)
-                pick[2 * q + c] = held[2 * p + c_src]
-
-                @pl.when(slot != me)
-                def _(slot=slot, c=c):
-                    remote(
-                        pick.at[2 * q + c],
-                        take.at[core * n + second],
-                        two_send.at[a],
-                        two_recv.at[a],
-                        (slot, here),
-                    ).start()
-
-            return 0
-
-        lax.fori_loop(0, n, choose, 0)
+        for k, (slot, origin) in enumerate(zip(slots, origins)):
+            pick[k] = held[origin]
+
+            @pl.when(slot != me)
+            def _(slot=slot, k=k):
+                remote(
+                    pick.at[k],
+                    take.at[core * n + second],
+                    two_send.at[a],
+                    two_recv.at[a],
+                    (slot, here),
+                ).start()
+
         take[core * n + second] = pick[2 * second + core]
 
     spread_state(0, stage_x, held_x)

time: 52.9 us -> 51.7 us (0.977)
  Pallas kernels: 47.9 us -> 46.7 us
    pallas_call x1, Pallas kernels: 47.9 us -> 46.7 us  [shards(): pl.pallas_call(functools.partial(kernel, n, nx), out_shape=(jax.ShapeDtyp...]
where the time goes in v3:
time: 51.7 us; the launch traced here: 51.5 us
  Pallas kernels  46.7 us (90%)
  between operations  2.98 us (6%)
  local copies, waits for them, and re-layouts  1.74 us (3%)
    pallas_call x1, Pallas kernels, shards(): pl.pallas_call(functools.partial(kernel, n, nx), out_shape=(jax.ShapeDtyp...  46.7 us
    unnamed x3, local copies, waits for them, and re-layouts  1.74 us

profile of v3, /device:TPU:1, one launch (start us, length us, event | category | flops | bytes accessed | tf_op | source)
XLA Modules:
  0.0 51.5 jit_solution(8605711729820058593)
XLA Ops:
  1.3 46.7 %shard_map.102 = (f32[1,32]{1,0:T(1,128)S(1)}, f32[3,24,128]{2,1,0:T(8,128)S(1)}, f32[3,24,128]{2,1,0:T(8,128)S(1)}, f32[1,1]{1,0:T(1,128)}) custom-call(f32[3,24,128]{2,1,0:T(8,128)} %bitcast.9, f32[3,24,128]{2,1,0:T(8,128)} %bitcast.10, f32[24,128]{1,0:T(8,128)} %bitcast.11, s32[24,27]{1,0:T(8,128)} %til_in.1, s32[1,128]{1,0:T(1,128)} %bitcast.12, ...), custom_call_target="tpu_custom_call" | custom-call | tf_op jit(solution)/shard_map/pallas_call | solution.py:559
  48.0 0.5 copy.20
  48.5 0.6 %copy.21 = f32[1,3,3072]{2,0,1:T(1,128)} copy(f32[1,3,3072]{2,0,1:T(1,128)S(1)} %bitcast.8) | data formatting | bytes 73728
  49.1 0.6 %copy.22 = f32[1,3,3072]{2,0,1:T(1,128)} copy(f32[1,3,3072]{2,0,1:T(1,128)S(1)} %bitcast.7) | data formatting | bytes 73728

commit v4 on v3

--- a/solution.py
+++ b/solution.py
@@ -84,6 +84,7 @@
     one_recv,
     two_send,
     two_recv,
+    far_recv,
 ):
     cells = pos.shape[1]
     members = 2 * n
@@ -337,19 +338,20 @@
     for copy in nexts:
         copy.start()
 
+    relay = n == 8
+
     def spread_state(a, stage, held):
         for h, own, low, step in ((0, zz, 2 * yy, members), (1, yy, zz * members + 1, 2)):
 
-            def send(p, h=h, own=own, low=low, step=step):
+            for k in (2, 6, 1, 7) if relay else range(1, n):
+                p = lax.rem(own + k, n)
                 remote(
                     stage.at[h],
                     held.at[2 * own + core],
                     one_send.at[a],
-                    one_recv.at[a],
+                    (far_recv if relay and k in (2, 6) else one_recv).at[a],
                     (low + p * step, here),
                 ).start()
-
-            others(n, own, send)
         remote(
             stage.at[pair],
             held.at[2 * second + core],
@@ -359,6 +361,22 @@
         ).start()
         held[2 * first + core] = stage[core]
 
+    def send_on(a, held):
+        if not relay:
+            return
+        wait_all(held.at[pl.ds(0, 4)], far_recv.at[a])
+        for away, near_step, c in ((2, 1, 0), (6, 7, 1)):
+            back = lax.rem(first + n - away, n)
+            for step, at, count in ((near_step, 2 * back, 2), (away, 2 * back + c, 1)):
+                p = lax.rem(first + step, n)
+                remote(
+                    held.at[pl.ds(at, count)],
+                    held.at[pl.ds(at, count)],
+                    one_send.at[a],
+                    one_recv.at[a],
+                    (p * first_stride + second * second_stride + core, here),
+                ).start()
+
     def source_of(slot):
         row = home[plan[slot]]
         return lax.div(row, members), lax.rem(lax.div(row, 2), n), lax.rem(row, 2)
@@ -372,7 +390,7 @@
             origins.append(2 * (z + core * (y - z)) + c_src)
 
     def hand_on(a, held, pick, take):
-        wait_all(held.at[pl.ds(0, members - 1)], one_recv.at[a])
+        wait_all(held.at[pl.ds(0, members - (5 if relay else 1))], one_recv.at[a])
 
         for k, (slot, origin) in enumerate(zip(slots, origins)):
             pick[k] = held[origin]
@@ -423,6 +441,14 @@
             share_features()
             hand_on(0, held_x, pick_x, take_x)
 
+        @pl.when(t == 4)
+        def _():
+            send_on(0, held_x)
+
+        @pl.when(t == pairs - 1)
+        def _():
+            send_on(1, held_va)
+
         p = jnp.where(t < near_pairs, (t + 1) % near_pairs, t)
         f = force(next_j, next_i, next_w, x1, p)
         for lane in range(2):
@@ -453,6 +479,7 @@
     lax.fori_loop(0, pairs, second_step, 0)
     spread_state(2, stage_vb, held_vb)
     hand_on(1, held_va, pick_va, take_va)
+    send_on(2, held_vb)
 
     wait_all(group.at[pl.ds(0, n - 1)], feat_recv.at[1])
     wide[...] = group[...].astype(jnp.float32).reshape(walkers, 3 * TILE)
@@ -470,7 +497,7 @@
 
     sums = lax.fori_loop(0, members, row_of, jnp.zeros((walkers, TILE), jnp.float32)).T
     for r in range(members):
-        part[r, :, 0:walkers] = jnp.broadcast_to(sums[r : r + 1], (8, walkers))
+        part[r, :, 0:walkers] = sums[r : r + 1]
     others(
         members,
         mine,
@@ -592,14 +619,14 @@
                 room(2, ROWS, TILE),
                 room(2, SPLIT, TILE),
                 room(2, ROWS - SPLIT, TILE),
-                room(cells, 8, TILE),
-                room(members, 8, TILE),
+                room(cells, 4, TILE),
+                room(members, 4, TILE),
                 room(n, members, 3 * TILE, kind=jnp.bfloat16),
                 room(walkers, 3 * TILE),
                 room(3, members, TILE),
-                room(members, 8, TILE),
-                room(members, 8, TILE),
-                room(nx, 8, TILE),
+                room(members, 1, TILE),
+                room(members, 1, TILE),
+                room(nx, 1, TILE),
                 room(members, ROWS, TILE),
                 room(members, SPLIT, TILE),
                 room(members, ROWS - SPLIT, TILE),
@@ -614,6 +641,7 @@
                 dma((6,)),
                 dma((4,)),
                 dma((4,)),
+                dma((3,)),
                 dma((3,)),
                 dma((3,)),
                 dma((3,)),

time: 51.7 us -> 54.3 us (1.050)
  Pallas kernels: 46.7 us -> 49.4 us
    pallas_call x1, Pallas kernels: 46.7 us -> 49.4 us  [shards(): pl.pallas_call(functools.partial(kernel, n, nx), out_shape=(jax.ShapeDtyp...]
where the time goes in v4:
time: 54.3 us; the launch traced here: 54.1 us
  Pallas kernels  49.4 us (91%)
  between operations  2.98 us (5%)
  local copies, waits for them, and re-layouts  1.74 us (3%)
    pallas_call x1, Pallas kernels, shards(): pl.pallas_call(functools.partial(kernel, n, nx), out_shape=(jax.ShapeDtyp...  49.4 us
    unnamed x3, local copies, waits for them, and re-layouts  1.74 us

profile of v4, /device:TPU:1, one launch (start us, length us, event | category | flops | bytes accessed | tf_op | source)
XLA Modules:
  0.0 54.1 jit_solution(2334654041206246)
XLA Ops:
  1.3 49.4 %shard_map.102 = (f32[1,32]{1,0:T(1,128)S(1)}, f32[3,24,128]{2,1,0:T(8,128)S(1)}, f32[3,24,128]{2,1,0:T(8,128)S(1)}, f32[1,1]{1,0:T(1,128)}) custom-call(f32[3,24,128]{2,1,0:T(8,128)} %bitcast.9, f32[3,24,128]{2,1,0:T(8,128)} %bitcast.10, f32[24,128]{1,0:T(8,128)} %bitcast.11, s32[24,27]{1,0:T(8,128)} %til_in.1, s32[1,128]{1,0:T(1,128)} %bitcast.12, ...), custom_call_target="tpu_custom_call" | custom-call | tf_op jit(solution)/shard_map/pallas_call | solution.py:586
  50.7 0.5 copy.20
  51.2 0.6 %copy.21 = f32[1,3,3072]{2,0,1:T(1,128)} copy(f32[1,3,3072]{2,0,1:T(1,128)S(1)} %bitcast.8) | data formatting | bytes 73728
  51.8 0.6 %copy.22 = f32[1,3,3072]{2,0,1:T(1,128)} copy(f32[1,3,3072]{2,0,1:T(1,128)S(1)} %bitcast.7) | data formatting | bytes 73728

commit v5 on v3

--- a/solution.py
+++ b/solution.py
@@ -223,7 +223,7 @@
         prepare_pair(pos, side_j, base_w, side_i, p)
         return 0
 
-    lax.fori_loop(0, cells // 2, prepare_own, 0)
+    lax.fori_loop(0, cells // 2, prepare_own, 0, unroll=4)
     for copy in loads[3:]:
         copy.wait()
 
@@ -306,34 +306,36 @@
     def order_one(t):
         return (t + 1) % pairs
 
-    def first_step(t, _):
-        @pl.when(t == 2)
+    def first_step(u, _):
+        @pl.when(u == 1)
         def _():
             pl.semaphore_wait(barrier, (nx - 1) + (members - 1) + 2 * (n - 1))
             for copy in halos:
                 copy.start()
 
-        @pl.when(t == pairs - 2)
+        @pl.when(u == pairs // 2 - 1)
         def _():
             for copy in halos:
                 copy.wait()
             prepare_halo(side_j, base_w, low_p, high_p)
 
-        p = order_one(t)
-        prepare_pair(x1, next_j, next_w, next_i, order_one(t + pairs - 1))
-        f = force(side_j, side_i, base_w, pos, p)
-        for lane in range(2):
-            g = 2 * p + lane
-            h, base, stride = stage_at(g)
-            for d in range(3):
-                v = vel[d, pl.ds(g, 1), :] + STEP * f[lane][d]
-                x = pos[d, pl.ds(g, 1), :] + STEP * v
-                v1[d, pl.ds(g, 1), :] = v
-                x1[d, pl.ds(g, 1), :] = x
-                stage_x[h, pl.ds(base + d * stride, 1), :] = x
+        now = [order_one(2 * u + k) for k in range(2)]
+        for k in range(2):
+            prepare_pair(x1, next_j, next_w, next_i, order_one(2 * u + k + pairs - 2))
+        both = [force(side_j, side_i, base_w, pos, p) for p in now]
+        for p, f in zip(now, both):
+            for lane in range(2):
+                g = 2 * p + lane
+                h, base, stride = stage_at(g)
+                for d in range(3):
+                    v = vel[d, pl.ds(g, 1), :] + STEP * f[lane][d]
+                    x = pos[d, pl.ds(g, 1), :] + STEP * v
+                    v1[d, pl.ds(g, 1), :] = v
+                    x1[d, pl.ds(g, 1), :] = x
+                    stage_x[h, pl.ds(base + d * stride, 1), :] = x
         return 0
 
-    lax.fori_loop(0, pairs, first_step, 0)
+    lax.fori_loop(0, pairs // 2, first_step, 0)
     for copy in nexts:
         copy.start()
 
@@ -390,7 +392,8 @@
         take[core * n + second] = pick[2 * second + core]
 
     spread_state(0, stage_x, held_x)
-    prepare_pair(x1, next_j, next_w, next_i, order_one(pairs - 1))
+    for k in range(2):
+        prepare_pair(x1, next_j, next_w, next_i, order_one(pairs - 2 + k))
 
     def share_features():
         feat_in[mine] = feat[mine]
@@ -407,50 +410,60 @@
 
     near_pairs = near // 2
 
-    def second_step(t, _):
-        @pl.when(t == near_pairs - 1)
+    def second_step(u, _):
+        @pl.when(u == near_pairs // 2 - 1)
         def _():
             for copy in nexts:
                 copy.wait()
             prepare_halo(next_j, next_w, low_n, high_n)
 
-        @pl.when(t == near_pairs)
+        @pl.when(u == near_pairs // 2)
         def _():
             spread_state(1, stage_va, held_va)
 
-        @pl.when(t == near_pairs + 1)
+        @pl.when(u == near_pairs // 2 + 1)
         def _():
             share_features()
             hand_on(0, held_x, pick_x, take_x)
 
-        p = jnp.where(t < near_pairs, (t + 1) % near_pairs, t)
-        f = force(next_j, next_i, next_w, x1, p)
-        for lane in range(2):
-            g = 2 * p + lane
-            h, base, stride = stage_at(g)
-            for d in range(3):
-                v = v1[d, pl.ds(g, 1), :] + STEP * f[lane][d]
-                x = x1[d, pl.ds(g, 1), :] + STEP * v
-
-                @pl.when(t < near_pairs)
-                def _(v=v, h=h, base=base, d=d):
-                    stage_va[h, pl.ds(base + 8 * d, 1), :] = v
-
-                @pl.when(t >= near_pairs)
-                def _(v=v, h=h, base=base, d=d):
-                    stage_vb[h, pl.ds(base - SPLIT + 4 * d, 1), :] = v
-
-                feat[g, pl.ds(d, 1), :] = x
-
-            @pl.when((g < members) & (g != mine))
-            def _(g=g):
-                remote(
-                    feat.at[g], feat_in.at[mine], feat_send.at[0], feat_recv.at[0], member(g)
-                ).start()
+        now = []
+        for k in range(2):
+            t = 2 * u + k
+            now.append(jnp.where(t < near_pairs, (t + 1) % near_pairs, t))
+        both = [force(next_j, next_i, next_w, x1, p) for p in now]
+        rows = []
+        for p, f in zip(now, both):
+            for lane in range(2):
+                g = 2 * p + lane
+                h, base, _ = stage_at(g)
+                for d in range(3):
+                    v = v1[d, pl.ds(g, 1), :] + STEP * f[lane][d]
+                    feat[g, pl.ds(d, 1), :] = x1[d, pl.ds(g, 1), :] + STEP * v
+                    rows.append((h, base, d, v))
+
+        @pl.when(u < near_pairs // 2)
+        def _():
+            for h, base, d, v in rows:
+                stage_va[h, pl.ds(base + 8 * d, 1), :] = v
+
+        @pl.when(u >= near_pairs // 2)
+        def _():
+            for h, base, d, v in rows:
+                stage_vb[h, pl.ds(base - SPLIT + 4 * d, 1), :] = v
+
+        for p in now:
+            for lane in range(2):
+                g = 2 * p + lane
+
+                @pl.when((g < members) & (g != mine))
+                def _(g=g):
+                    remote(
+                        feat.at[g], feat_in.at[mine], feat_send.at[0], feat_recv.at[0], member(g)
+                    ).start()
 
         return 0
 
-    lax.fori_loop(0, pairs, second_step, 0)
+    lax.fori_loop(0, pairs // 2, second_step, 0)
     spread_state(2, stage_vb, held_vb)
     hand_on(1, held_va, pick_va, take_va)
 

time: 51.7 us -> 51.1 us (0.988)
    pallas_call x1, Pallas kernels: 46.7 us -> 46.2 us  [shards(): pl.pallas_call(functools.partial(kernel, n, nx), out_shape=(jax.ShapeDtyp...]
where the time goes in v5:
time: 51.1 us; the launch traced here: 50.9 us
  Pallas kernels  46.2 us (90%)
  between operations  2.98 us (6%)
  local copies, waits for them, and re-layouts  1.74 us (3%)
    pallas_call x1, Pallas kernels, shards(): pl.pallas_call(functools.partial(kernel, n, nx), out_shape=(jax.ShapeDtyp...  46.2 us
    unnamed x3, local copies, waits for them, and re-layouts  1.74 us

profile of v5, /device:TPU:1, one launch (start us, length us, event | category | flops | bytes accessed | tf_op | source)
XLA Modules:
  0.0 50.9 jit_solution(16930662105695261153)
XLA Ops:
  1.3 46.2 %shard_map.102 = (f32[1,32]{1,0:T(1,128)S(1)}, f32[3,24,128]{2,1,0:T(8,128)S(1)}, f32[3,24,128]{2,1,0:T(8,128)S(1)}, f32[1,1]{1,0:T(1,128)}) custom-call(f32[3,24,128]{2,1,0:T(8,128)} %bitcast.9, f32[3,24,128]{2,1,0:T(8,128)} %bitcast.10, f32[24,128]{1,0:T(8,128)} %bitcast.11, s32[24,27]{1,0:T(8,128)} %til_in.1, s32[1,128]{1,0:T(1,128)} %bitcast.12, ...), custom_call_target="tpu_custom_call" | custom-call | tf_op jit(solution)/shard_map/pallas_call | solution.py:572
  47.5 0.5 %copy.20 = f32[1,32]{1,0:T(1,128)} copy(f32[1,32]{1,0:T(1,128)S(1)} %get-tuple-element.24) | data formatting | bytes 256
  48.0 0.6 %copy.21 = f32[1,3,3072]{2,0,1:T(1,128)} copy(f32[1,3,3072]{2,0,1:T(1,128)S(1)} %bitcast.8) | data formatting | bytes 73728
  48.6 0.6 %copy.22 = f32[1,3,3072]{2,0,1:T(1,128)} copy(f32[1,3,3072]{2,0,1:T(1,128)S(1)} %bitcast.7) | data formatting | bytes 73728
